TPU v7x, 32 devices: a whole 2x2x4 slice. The times are simulated.
32 devices in a mesh: tm: 4 (over y, x), stn: 8 (over z, core).
Axes of the slice: x: 2, y: 2, z: 4, core: 2. Of those that a mesh axis runs over, the one named last changes fastest.
Arguments:
- voltages: bfloat16 [256, 262144], P('stn', 'tm'), may hold values from -6 to 6
- gains: float32 [2, 256, 256], P(None, 'stn'), may hold values from -4 to 4
Outputs:
- visibility: float32 [256, 2, 256, 256], P(('tm', 'stn'))
All inputs are finite; a program needn't handle non-finite values.
Results may differ from a plain program's by a relative error of at most 0.0038.
Values may be sent and summed in bfloat16 or wider, within the bound.
A program may use at most 128 MiB of HBM per device.

v0:
```python
import jax
import jax.numpy as jnp
from jax import lax
from jax.sharding import PartitionSpec as P

CHANNELS = 4096
BAND_LOW = 1024
TAPS = 8


def passed_along(x, axis, by):
    devices = lax.axis_size(axis)
    pairs = [(i, i + by) for i in range(devices) if 0 <= i + by < devices]
    return lax.ppermute(x, axis, pairs)


def window_table(chans):
    frame_len = 2 * chans
    total_len = TAPS * frame_len
    positions = jnp.arange(total_len, dtype=jnp.float32)
    centred = (positions - (total_len - 1) / 2.0) / frame_len
    taper = jnp.sin(jnp.pi * (positions + 0.5) / total_len)
    shaped = jnp.sinc(centred) * taper * taper
    shaped = shaped / jnp.sqrt(jnp.sum(shaped * shaped))
    return shaped.reshape(TAPS, frame_len)


def band_tables(frame_len, band):
    sample_index = jnp.arange(frame_len, dtype=jnp.int32)[:, None]
    channel_index = (BAND_LOW + jnp.arange(band, dtype=jnp.int32))[None, :]
    phase = (sample_index * channel_index % frame_len).astype(jnp.float32)
    angles = 2.0 * jnp.pi * phase / frame_len
    return (jnp.cos(angles), jnp.sin(angles))


def band_spectra(windowed, cos_table, sin_table):
    highest = lax.Precision.HIGHEST
    real_part = jnp.einsum("ifm,mk->kif", windowed, cos_table, precision=highest)
    imag_part = -jnp.einsum("ifm,mk->kif", windowed, sin_table, precision=highest)
    return (real_part, imag_part)


def apply_taps(window, extended, frames):
    windowed = jnp.zeros((extended.shape[0], frames, extended.shape[2]), jnp.float32)
    for tap_index in range(TAPS):
        windowed = windowed + window[tap_index] * extended[
            :, tap_index : tap_index + frames, :
        ].astype(jnp.float32)
    return windowed


def operands(turned):
    stacked = jnp.concatenate([turned[0], turned[1]], axis=-1)
    flipped = jnp.concatenate([turned[1], -turned[0]], axis=-1)
    return (stacked, flipped)


def cross_power(stacked, flipped, total_frames):
    vis_real = jnp.einsum("cif,cjf->cij", stacked, stacked, preferred_element_type=jnp.float32)
    vis_imag = jnp.einsum("cif,cjf->cij", flipped, stacked, preferred_element_type=jnp.float32)
    return jnp.stack([vis_real, vis_imag], axis=1) / total_frames


def on_device(voltages, gains):
    in_dev, length = voltages.shape
    band = gains.shape[2]
    frame_len = 2 * CHANNELS
    frames = length // frame_len
    n_time = lax.axis_size("tm")
    n_station = lax.axis_size("stn")
    per_device = band // (n_time * n_station)
    all_inputs = in_dev * n_station
    history = TAPS - 1
    window = window_table(CHANNELS)
    cos_table, sin_table = band_tables(frame_len, band)
    framed = voltages.reshape(in_dev, frames, frame_len)
    before = passed_along(framed[:, frames - history :, :], "tm", 1)
    extended = jnp.concatenate([before, framed], axis=1)
    windowed = apply_taps(window, extended, frames)
    raw_real, raw_imag = band_spectra(windowed, cos_table, sin_table)
    gain_real = jnp.transpose(gains[0])[:, :, None]
    gain_imag = jnp.transpose(gains[1])[:, :, None]
    spec_real = gain_real * raw_real - gain_imag * raw_imag
    spec_imag = gain_real * raw_imag + gain_imag * raw_real
    spectra = jnp.stack([spec_real, spec_imag]).astype(jnp.bfloat16)
    blocks = spectra.reshape(2, n_time, n_station, per_device, in_dev, frames)
    turned = lax.all_to_all(
        lax.all_to_all(blocks, "tm", split_axis=1, concat_axis=5, tiled=True),
        "stn",
        split_axis=2,
        concat_axis=4,
        tiled=True,
    )
    turned = turned.reshape(2, per_device, all_inputs, n_time * frames)
    stacked, flipped = operands(turned)
    return cross_power(stacked, flipped, float(n_time * frames))


def solution(mesh):
    in_specs = (P("stn", "tm"), P(None, "stn", None))
    out_specs = P(("tm", "stn"), None, None, None)
    return jax.shard_map(
        on_device, mesh=mesh, in_specs=in_specs, out_specs=out_specs, check_vma=False
    )
```

profile of v0, /device:TPU:0, one launch (start us, length us, event | category | flops | bytes accessed | tf_op | source)
XLA Modules:
  0.0 210.4 jit_solution(2259311933544626942)
XLA Ops:
  0.0 0.0 copy-start.1
  0.0 2.5 %copy.37 = bf16[4,8,8,8192]{3,2,0,1:T(8,128)(2,1)S(1)} copy(bf16[4,8,8,8192]{3,2,1,0:T(8,128)(2,1)} %bitcast.66) | data formatting | bytes 8388608 | tf_op jit(solution)/shard_map/reshape | solution.py:76
  2.5 2.1 slice.93
  4.6 6.6 %collective-permute-start = (bf16[32,7,8192]{2,0,1:T(8,128)(2,1)}, bf16[32,7,8192]{2,0,1:T(8,128)(2,1)}, u32[]{:S(2)}, u32[]{:S(2)}) collective-permute-start(bf16[32,7,8192]{2,0,1:T(8,128)(2,1)} %slice.93), channel_id=1, source_target_pairs={{0,8},{8,16},{16,24},{1,9},{9,17},{17,25},{2,10},{10,18},{18,26},{... | collective-permute-start | bytes 11010056 | tf_op jit(solution)/shard_map/ppermute | solution.py:14
  11.2 1.8 multiply_reduce_fusion
  13.6 0.0 copy-start
  13.7 0.0 copy-done.1
  13.7 1.2 broadcast_divide_fusion
  15.0 73.4 %collective-permute-done = bf16[32,7,8192]{2,0,1:T(8,128)(2,1)} collective-permute-done((bf16[32,7,8192]{2,0,1:T(8,128)(2,1)}, bf16[32,7,8192]{2,0,1:T(8,128)(2,1)}, u32[]{:S(2)}, u32[]{:S(2)}) %collective-permute-start) | collective-permute-done | bytes 3670048 | tf_op jit(solution)/shard_map/ppermute | solution.py:14
  88.3 2.3 %constant_dynamic-update-slice_fusion.1 = bf16[32,15,8192]{2,0,1:T(8,128)(2,1)S(1)} fusion(bf16[32,7,8192]{2,0,1:T(8,128)(2,1)} %collective-permute-done), kind=kLoop, calls=%fused_computation.68 | loop fusion | bytes 7340032
  90.6 0.0 copy-done
  90.6 0.4 constant_dynamic-update-slice_fusion
  91.0 7.9 %multiply_add_fusion = f32[32,8,8192]{2,0,1:T(8,128)S(1)} fusion(bf16[32,15,8192]{2,0,1:T(8,128)(2,1)S(1)} %constant_dynamic-update-slice_fusion, f32[8192]{0:T(1024)S(1)} %get-tuple-element.10, f32[8192]{0:T(1024)S(1)} %get-tuple-element.11, f32[8192]{0:T(1024)S(1)} %get-tuple-element.12, f32[8192]{0:T(1024)S(1)} %get-tuple-element.13, ...), kind=kLoop, calls=%fused_computation.11 | loop fusion | flops 48234496 | bytes 42205184 | tf_op jit(solution)/shard_map/add | solution.py:46
  99.0 38.5 %fusion.5 = f32[256,32,8]{0,1,2:T(8,128)S(1)} fusion(f32[32,8,8192]{2,0,1:T(8,128)S(1)} %multiply_add_fusion, s32[256]{0:T(256)S(1)} %iota_add_fusion.2), kind=kOutput, calls=%fused_computation.8 | convolution fusion | flops 6471811072 | bytes 8651776 | tf_op jit(solution)/shard_map/ifm,mk->kif/dot_general | solution.py:38
  137.4 38.8 %subtract_convert_fusion = (bf16[256,32,8]{0,1,2:T(8,128)(2,1)S(1)}, bf16[256,32,8]{0,1,2:T(8,128)(2,1)S(1)}) fusion(f32[256,32,8]{0,1,2:T(8,128)S(1)} %fusion.5, f32[256,32]{0,1:T(8,128)S(1)} %get-tuple-element.20, f32[256,32]{0,1:T(8,128)S(1)} %get-tuple-element.19, f32[32,8,8192]{2,0,1:T(8,128)S(1)} %multiply_add_fusion, s32[256]{0:T(256)S(1)} %iota_add_fusion.2), kind=kOutput, calls=%fused_computation.62 | convolution fusion | flops 6472400896 | bytes 8979456 | tf_op jit(solution)/shard_map/ifm,mk->kif/dot_general | solution.py:39
  176.3 0.3 copy.19
  176.6 0.3 copy.20
  176.9 0.3 copy_bitcast_fusion.3
  177.2 1.0 reshape.50
  178.2 10.2 %all_to_all.33 = bf16[4,2,16384]{2,1,0:T(2,128)(2,1)S(1)} all-to-all(bf16[4,2,16384]{2,1,0:T(2,128)(2,1)S(1)} %reshape.50), channel_id=1, replica_groups=mesh['tm'=4,'stn'=8] {'tm'}, dimensions={0} | all-to-all | bytes 524288 | tf_op jit(solution)/shard_map/all_to_all | solution.py:88
  188.4 0.5 reshape.51
  188.9 0.2 copy_bitcast_fusion.2
  189.1 1.0 reshape.52
  190.1 14.4 %all_to_all.34 = bf16[8,2,8192]{2,1,0:T(2,128)(2,1)S(1)} all-to-all(bf16[8,2,8192]{2,1,0:T(2,128)(2,1)S(1)} %reshape.52), channel_id=1, replica_groups=mesh['tm'=4,'stn'=8] {'stn'}, dimensions={0} | all-to-all | bytes 524288 | tf_op jit(solution)/shard_map/all_to_all | solution.py:87
  204.5 0.5 reshape.53
  205.0 0.1 bitcast_bitcast_fusion
  205.1 0.1 fusion.55
  205.2 0.3 copy.24
  205.6 0.4 squeeze.16
  205.9 0.3 copy.25
  206.3 0.4 squeeze.17
  206.7 0.5 convolution_bitcast_fusion.1
  207.2 0.5 convolution_bitcast_fusion
  207.6 0.3 maximum_multiply_fusion
  208.0 2.4 %copy.26 = f32[8,2,256,256]{3,2,1,0:T(8,128)} copy(f32[8,2,256,256]{3,2,0,1:T(8,128)S(1)} %maximum_multiply_fusion) | data formatting | bytes 8388608 | tf_op jit(solution)/shard_map/div | solution.py:61
  (5 shorter events, 0.1 us)
Async XLA Ops:
  0.0 13.7 %copy-start.1 = (f32[2,32,256]{2,1,0:T(8,128)S(1)}, f32[2,32,256]{2,1,0:T(8,128)}, u32[]{:S(2)}) copy-start(f32[2,32,256]{2,1,0:T(8,128)} %param.3) | copy-start | bytes 196612
  4.6 83.7 %collective-permute-start = (bf16[32,7,8192]{2,0,1:T(8,128)(2,1)}, bf16[32,7,8192]{2,0,1:T(8,128)(2,1)}, u32[]{:S(2)}, u32[]{:S(2)}) collective-permute-start(bf16[32,7,8192]{2,0,1:T(8,128)(2,1)} %slice.93), channel_id=1, source_target_pairs={{0,8},{8,16},{16,24},{1,9},{9,17},{17,25},{2,10},{10,18},{18,26},{... | collective-permute-start | bytes 11010056 | tf_op jit(solution)/shard_map/ppermute | solution.py:14
  13.6 77.0 %copy-start = (bf16[32,65536]{1,0:T(8,128)(2,1)S(1)}, bf16[32,65536]{1,0:T(8,128)(2,1)}, u32[]{:S(2)}) copy-start(bf16[32,65536]{1,0:T(8,128)(2,1)} %param.2) | copy-start | bytes 12582916
where the time goes:
time: 211 us; the launch traced here: 210 us
  matrix products  78.2 us (37%)
  waiting for transfers between devices  73.4 us (35%)
  blocking collectives  24.6 us (12%)
  local copies, waits for them, and re-layouts  15.1 us (7%)
  other arithmetic  11.7 us (6%)
  starting transfers between devices  6.63 us (3%)
    ppermute x1, waiting for transfers between devices, passed_along(): return lax.ppermute(x, axis, pairs)  73.4 us
    dot_general x1, matrix products, band_spectra(): jnp.einsum('ifm,mk->kif', windowed, sin_table, precision=highest)  38.8 us
    dot_general x1, matrix products, band_spectra(): jnp.einsum('ifm,mk->kif', windowed, cos_table, precision=highest)  38.5 us
    all_to_all x1, blocking collectives, on_device(): lax.all_to_all(lax.all_to_all(blocks, 'tm', split_axis=1, concat_axis=5,...  14.4 us
    all_to_all x1, blocking collectives, on_device(): lax.all_to_all(blocks, 'tm', split_axis=1, concat_axis=5, tiled=True)  10.2 us
    add x1, other arithmetic, apply_taps(): windowed + window[tap_index] * extended[:, tap_index:tap_index + frames,...  7.9 us
    ppermute x1, starting transfers between devices, passed_along(): return lax.ppermute(x, axis, pairs)  6.63 us
    unnamed x10, local copies, waits for them, and re-layouts  5.38 us
  transfers between devices with their start and end apart: 1, of which 1 were waited for; matrix products, arithmetic and copies ran while one was open for 1% of the time, Pallas kernels for 0%

commit v1 on v0

--- a/solution.py
+++ b/solution.py
@@ -1,6 +1,11 @@
+import functools
+
 import jax
 import jax.numpy as jnp
+import numpy as np
 from jax import lax
+from jax.experimental import pallas as pl
+from jax.experimental.pallas import tpu as pltpu
 from jax.sharding import PartitionSpec as P
 
 CHANNELS = 4096
@@ -96,9 +101,354 @@
     return cross_power(stacked, flipped, float(n_time * frames))
 
 
+HALO = jnp.float32
+CHUNK = 512
+LANES = 128
+
+
+def host_window(chans):
+    frame_len = 2 * chans
+    total = TAPS * frame_len
+    n = np.arange(total, dtype=np.float64)
+    raw = np.sinc((n - (total - 1) / 2) / frame_len)
+    raw = raw * np.sin(np.pi * (n + 0.5) / total) ** 2
+    return (raw / np.sqrt(np.sum(raw * raw))).reshape(TAPS, frame_len).astype(np.float32)
+
+
+def host_tables(chans, band, owners):
+    frame_len = 2 * chans
+    m = np.arange(chans, dtype=np.int64)[:, None]
+    parts = []
+    for parity in range(2):
+        c = BAND_LOW + np.arange(parity, band, 2, dtype=np.int64)[None, :]
+        angle = 2.0 * np.pi * ((m * c) % frame_len) / frame_len
+        parts.append(np.concatenate([np.cos(angle), -np.sin(angle)], axis=1))
+    full = np.stack(parts)
+    high = full.astype(np.float32).astype(jnp.bfloat16)
+    low = (full - high.astype(np.float64)).astype(np.float32).astype(jnp.bfloat16)
+    return np.stack([high, low])
+
+
+def taps_into(v_ref, w_ref, x_ref, base, in_dev, frames, halo):
+    rows = in_dev * (frames - 1 if halo else frames)
+    for tile in range(CHUNK // LANES):
+        at = pl.multiple_of(base + tile * LANES, LANES)
+        here = slice(tile * LANES, (tile + 1) * LANES)
+        for part in range(in_dev // 16):
+            who = slice(part * 16, part * 16 + 16)
+            halves = []
+            for half in range(2):
+                v = [
+                    v_ref[2 * f + half, who, pl.ds(at, LANES)].astype(jnp.float32)
+                    for f in range(frames)
+                ]
+                w = [w_ref[half, pl.ds(p, 1), pl.ds(at, LANES)] for p in range(TAPS)]
+                sums = []
+                if halo:
+                    for j in range(frames - 1):
+                        sums.append(sum(w[p] * v[j + 1 + p] for p in range(TAPS - 1 - j)))
+                else:
+                    for f in range(frames):
+                        sums.append(sum(w[TAPS - 1 - q] * v[f - q] for q in range(f + 1)))
+                halves.append(sums)
+            for f in range(len(halves[0])):
+                for parity in range(2):
+                    a, b = halves[0][f], halves[1][f]
+                    x = a - b if parity else a + b
+                    high = x.astype(jnp.bfloat16)
+                    low = (x - high.astype(jnp.float32)).astype(jnp.bfloat16)
+                    r = f * in_dev + part * 16
+                    x_ref[parity, r : r + 16, here] = high
+                    x_ref[parity, rows + r : rows + r + 16, here] = low
+
+
+def transform(x_ref, t_ref, acc_ref, base, rows):
+    at = pl.multiple_of(base, CHUNK)
+    for parity in range(2):
+        x = x_ref[parity, 0 : 2 * rows, :]
+        th = t_ref[0, parity, pl.ds(at, CHUNK), :]
+        tl = t_ref[1, parity, pl.ds(at, CHUNK), :]
+        both = jnp.dot(x, th, preferred_element_type=jnp.float32)
+        extra = jnp.dot(x[:rows], tl, preferred_element_type=jnp.float32)
+        acc_ref[parity, 0:rows, :] += both[:rows] + both[rows:] + extra
+
+
+def swap_blocks(arrays, block):
+    lane = lax.broadcasted_iota(jnp.int32, arrays[0].shape, 1)
+    step = 1
+    while step < len(arrays):
+        low = (lane // (block * step)) % 2 == 0
+        shift = block * step
+        out = list(arrays)
+        for q in range(len(arrays)):
+            if q & step == 0:
+                a, b = arrays[q], arrays[q | step]
+                out[q] = jnp.where(low, a, pltpu.roll(b, shift, 1))
+                out[q | step] = jnp.where(low, pltpu.roll(a, LANES - shift, 1), b)
+        arrays = out
+        step *= 2
+    return arrays
+
+
+def spectra_kernel(
+    n_time, n_station, frames,
+    v_hbm, w_hbm, t_hbm, g_ref, got_ref,
+    v_ref, w_ref, t_ref, x0, x1, acc, hsend, hrecv, send, gain,
+    v_sem, w_sem, t_sem, h_sem, send_sem, recv_sem,
+):
+    me_t, me_s = lax.axis_index("tm"), lax.axis_index("stn")
+    n_dev = n_time * n_station
+    me = me_t * n_station + me_s
+    in_dev, half_len = v_ref.shape[1], v_ref.shape[2]
+    chunks = half_len // CHUNK
+    barrier = pltpu.get_barrier_semaphore()
+
+    def greet(o, carry):
+        to = lax.rem(me + o, n_dev)
+        pl.semaphore_signal(
+            barrier, inc=1, device_id=(to // n_station, lax.rem(to, n_station)),
+            device_id_type=pl.DeviceIdType.MESH,
+        )
+        return carry
+
+    lax.fori_loop(1, n_dev, greet, 0)
+
+    def v_copy(c, i):
+        at = pl.multiple_of(c * CHUNK, CHUNK)
+        src = pl.multiple_of(i * half_len + c * CHUNK, CHUNK)
+        return pltpu.make_async_copy(
+            v_hbm.at[:, pl.ds(src, CHUNK)], v_ref.at[i, :, pl.ds(at, CHUNK)], v_sem.at[c, i]
+        )
+
+    def t_copy(c):
+        at = pl.multiple_of(c * CHUNK, CHUNK)
+        return pltpu.make_async_copy(
+            t_hbm.at[:, :, pl.ds(at, CHUNK), :], t_ref.at[:, :, pl.ds(at, CHUNK), :], t_sem.at[c]
+        )
+
+    w_copy = pltpu.make_async_copy(w_hbm, w_ref, w_sem)
+    w_copy.start()
+
+    def begin(c, carry):
+        lax.fori_loop(0, 2 * frames, lambda i, k: (v_copy(c, i).start(), k)[1], 0)
+        t_copy(c).start()
+        return carry
+
+    lax.fori_loop(0, chunks, begin, 0)
+    acc[...] = jnp.zeros_like(acc)
+
+    def arrived(c):
+        lax.fori_loop(0, 2 * frames, lambda i, k: (v_copy(c, i).wait(), k)[1], 0)
+        t_copy(c).wait()
+
+    def sweep(halo):
+        rows = in_dev * (frames - 1 if halo else frames)
+
+        def taps(c, x):
+            taps_into(v_ref, w_ref, x, c * CHUNK, in_dev, frames, halo)
+
+        if halo:
+            arrived(0)
+        taps(0, x0)
+
+        def pair(k, carry):
+            c = 2 * k
+            if halo:
+                arrived(c + 1)
+
+                @pl.when(c + 2 < chunks)
+                def _():
+                    arrived(c + 2)
+
+            taps(c + 1, x1)
+            transform(x0, t_ref, acc, c * CHUNK, rows)
+            taps(jnp.minimum(c + 2, chunks - 1), x0)
+            transform(x1, t_ref, acc, (c + 1) * CHUNK, rows)
+            return carry
+
+        lax.fori_loop(0, chunks // 2, pair, 0)
+
+    w_copy.wait()
+    sweep(True)
+    hrows = in_dev * (frames - 1)
+    for parity in range(2):
+        hsend[parity] = acc[parity, 0:hrows, :].astype(hsend.dtype)
+    pl.semaphore_wait(barrier, n_dev - 1)
+    onward = pltpu.make_async_remote_copy(
+        src_ref=hsend, dst_ref=hrecv, send_sem=h_sem.at[0], recv_sem=h_sem.at[1],
+        device_id=(lax.rem(me_t + 1, n_time), me_s), device_id_type=pl.DeviceIdType.MESH,
+    )
+
+    @pl.when(me_t < n_time - 1)
+    def _():
+        onward.start()
+
+    acc[...] = jnp.zeros_like(acc)
+    band = g_ref.shape[2]
+    row = lax.broadcasted_iota(jnp.int32, (band, band), 0)
+    col = lax.broadcasted_iota(jnp.int32, (band, band), 1)
+    pick = (row == 2 * lax.rem(col, band // 2) + col // (band // 2)).astype(jnp.float32)
+    for reim in range(2):
+        gain[reim] = jnp.dot(
+            g_ref[reim], pick, precision=lax.Precision.HIGHEST, preferred_element_type=jnp.float32
+        )
+    sweep(False)
+
+    @pl.when(me_t > 0)
+    def _():
+        onward.wait_recv()
+        for parity in range(2):
+            acc[parity, 0:hrows, :] += hrecv[parity].astype(jnp.float32)
+
+    half = band // 2
+    for part in range(in_dev // 16):
+        who = slice(part * 16, part * 16 + 16)
+        arrays = []
+        for parity in range(2):
+            gr = gain[0, who, parity * half : (parity + 1) * half]
+            gi = gain[1, who, parity * half : (parity + 1) * half]
+            res, ims = [], []
+            for f in range(frames):
+                r = f * in_dev + part * 16
+                re = acc[parity, r : r + 16, 0:half]
+                im = acc[parity, r : r + 16, half:band]
+                res.append(gr * re - gi * im)
+                ims.append(gr * im + gi * re)
+            arrays += res + ims
+        arrays = swap_blocks(arrays, LANES // len(arrays))
+        for d in range(n_dev):
+            send[d, who, :] = arrays[d].astype(jnp.bfloat16)
+    got_ref[me] = send[me]
+
+    def outgoing(o):
+        to = lax.rem(me + o, n_dev)
+        return pltpu.make_async_remote_copy(
+            src_ref=send.at[to], dst_ref=got_ref.at[me],
+            send_sem=send_sem.at[o], recv_sem=recv_sem.at[me],
+            device_id=(to // n_station, lax.rem(to, n_station)),
+            device_id_type=pl.DeviceIdType.MESH,
+        )
+
+    def incoming(o):
+        src = lax.rem(me + o, n_dev)
+        return pltpu.make_async_remote_copy(
+            src_ref=send.at[src], dst_ref=got_ref.at[src],
+            send_sem=send_sem.at[o], recv_sem=recv_sem.at[src],
+            device_id=(src // n_station, lax.rem(src, n_station)),
+            device_id_type=pl.DeviceIdType.MESH,
+        )
+
+    lax.fori_loop(1, n_dev, lambda o, k: (outgoing(o).start(), k)[1], 0)
+    lax.fori_loop(1, n_dev, lambda o, k: (incoming(o).wait_recv(), k)[1], 0)
+    lax.fori_loop(1, n_dev, lambda o, k: (outgoing(o).wait_send(), k)[1], 0)
+
+    @pl.when(me_t < n_time - 1)
+    def _():
+        onward.wait_send()
+
+
+def correlate_kernel(n_time, got_ref, out_ref, a_ref, b_ref):
+    c = pl.program_id(0)
+    inputs = out_ref.shape[2]
+    reach = LANES // 4
+
+    @pl.when(c == 0)
+    def _():
+        for t in range(n_time):
+            here = slice(t * LANES, (t + 1) * LANES)
+            a = got_ref[t * inputs : (t + 1) * inputs, :]
+            wide = a.astype(jnp.float32)
+            lane = lax.broadcasted_iota(jnp.int32, wide.shape, 1)
+            real = (lane // reach) % 2 == 0
+            turned = jnp.where(
+                real, pltpu.roll(wide, LANES - reach, 1), -pltpu.roll(wide, reach, 1)
+            )
+            a_ref[0:inputs, here] = a
+            a_ref[inputs : 2 * inputs, here] = turned.astype(jnp.bfloat16)
+
+    lane = lax.rem(lax.broadcasted_iota(jnp.int32, (1, n_time * LANES), 1), LANES)
+    mine = (lane // (LANES // 2) == lax.rem(c, 2)) & (lax.rem(lane, 4) == c // 2)
+    mask = jnp.where(mine, 1.0, 0.0).astype(jnp.bfloat16)
+    b_ref[...] = a_ref[0:inputs, :] * mask
+    power = lax.dot_general(
+        a_ref[...], b_ref[...], (((1,), (1,)), ((), ())), preferred_element_type=jnp.float32
+    )
+    power = power * (1.0 / (8 * n_time))
+    out_ref[0, 0] = power[:inputs]
+    out_ref[0, 1] = power[inputs:]
+
+
+def on_device_fast(voltages, gains):
+    in_dev, length = voltages.shape
+    band = gains.shape[2]
+    frame_len = 2 * CHANNELS
+    frames = length // frame_len
+    n_time = lax.axis_size("tm")
+    n_station = lax.axis_size("stn")
+    n_dev = n_time * n_station
+    inputs = in_dev * n_station
+    hrows = in_dev * (frames - 1)
+    rows = in_dev * frames
+    window = host_window(CHANNELS).reshape(TAPS, 2, CHANNELS).transpose(1, 0, 2)
+    tables = host_tables(CHANNELS, band, n_dev)
+    chunks = CHANNELS // CHUNK
+    any_space = pl.BlockSpec(memory_space=pl.ANY)
+    vmem = pl.BlockSpec(memory_space=pltpu.VMEM)
+    got = pl.pallas_call(
+        functools.partial(spectra_kernel, n_time, n_station, frames),
+        out_shape=jax.ShapeDtypeStruct((n_dev, in_dev, LANES), jnp.bfloat16),
+        in_specs=[any_space, any_space, any_space, vmem],
+        out_specs=vmem,
+        scratch_shapes=[
+            pltpu.VMEM((2 * frames, in_dev, CHANNELS), jnp.bfloat16),
+            pltpu.VMEM((2, TAPS, CHANNELS), jnp.float32),
+            pltpu.VMEM((2, 2, CHANNELS, band), jnp.bfloat16),
+            pltpu.VMEM((2, 2 * rows, CHUNK), jnp.bfloat16),
+            pltpu.VMEM((2, 2 * rows, CHUNK), jnp.bfloat16),
+            pltpu.VMEM((2, rows, band), jnp.float32),
+            pltpu.VMEM((2, hrows, band), HALO),
+            pltpu.VMEM((2, hrows, band), HALO),
+            pltpu.VMEM((n_dev, in_dev, LANES), jnp.bfloat16),
+            pltpu.VMEM((2, in_dev, band), jnp.float32),
+            pltpu.SemaphoreType.DMA((chunks, 2 * frames)),
+            pltpu.SemaphoreType.DMA,
+            pltpu.SemaphoreType.DMA((chunks,)),
+            pltpu.SemaphoreType.DMA((2,)),
+            pltpu.SemaphoreType.DMA((n_dev,)),
+            pltpu.SemaphoreType.DMA((n_dev,)),
+        ],
+        compiler_params=pltpu.CompilerParams(
+            collective_id=0, has_side_effects=True, vmem_limit_bytes=48 * 2**20
+        ),
+        name="spectra",
+    )(voltages, window, tables, gains)
+    per_device = band // n_dev
+    return pl.pallas_call(
+        functools.partial(correlate_kernel, n_time),
+        grid=(per_device,),
+        out_shape=jax.ShapeDtypeStruct((per_device, 2, inputs, inputs), jnp.float32),
+        in_specs=[pl.BlockSpec((n_time * inputs, LANES), lambda c: (0, 0))],
+        out_specs=pl.BlockSpec((1, 2, inputs, inputs), lambda c: (c, 0, 0, 0)),
+        scratch_shapes=[
+            pltpu.VMEM((2 * inputs, n_time * LANES), jnp.bfloat16),
+            pltpu.VMEM((inputs, n_time * LANES), jnp.bfloat16),
+        ],
+        compiler_params=pltpu.CompilerParams(vmem_limit_bytes=32 * 2**20),
+        name="correlate",
+    )(got.reshape(n_time * inputs, LANES))
+
+
 def solution(mesh):
     in_specs = (P("stn", "tm"), P(None, "stn", None))
     out_specs = P(("tm", "stn"), None, None, None)
+
+    def body(voltages, gains):
+        n_dev = mesh.shape["tm"] * mesh.shape["stn"]
+        frames = voltages.shape[1] // (2 * CHANNELS)
+        if 2 * frames * (gains.shape[2] // n_dev) == LANES and frames == TAPS:
+            return on_device_fast(voltages, gains)
+        return on_device(voltages, gains)
+
     return jax.shard_map(
-        on_device, mesh=mesh, in_specs=in_specs, out_specs=out_specs, check_vma=False
+        body, mesh=mesh, in_specs=in_specs, out_specs=out_specs, check_vma=False
     )

time: 211 us -> 43.9 us (0.21)
  matrix products: 78.2 us -> 0 us
  waiting for transfers between devices: 73.4 us -> 0 us
  Pallas kernels: 0 us -> 39.7 us
  blocking collectives: 24.6 us -> 0 us
  other arithmetic: 11.7 us -> 0 us
  local copies, waits for them, and re-layouts: 15.1 us -> 3.98 us
  starting transfers between devices: 6.63 us -> 0 us
    dot_general x4 -> x0, matrix products: 78.2 us -> none  [the longest x1 38.8 us: band_spectra(): jnp.einsum('ifm,mk->kif', windowed, sin_table, precision=highest)]
    ppermute x1 -> x0, waiting for transfers between devices: 73.4 us -> none  [passed_along(): return lax.ppermute(x, axis, pairs)]
    pallas_call x0 -> x2, Pallas kernels: none -> 39.7 us  [the longest x1 34.5 us: on_device_fast(): pl.pallas_call(functools.partial(spectra_kernel, n_time, n_station, frame...]
    all_to_all x2 -> x0, blocking collectives: 24.6 us -> none  [the longest x1 14.4 us: on_device(): lax.all_to_all(lax.all_to_all(blocks, 'tm', split_axis=1, concat_axis=5,...]
    add x2 -> x0, other arithmetic: 7.91 us -> none  [the longest x1 7.9 us: apply_taps(): windowed + window[tap_index] * extended[:, tap_index:tap_index + frames,...]
    ppermute x1 -> x0, starting transfers between devices: 6.63 us -> none  [passed_along(): return lax.ppermute(x, axis, pairs)]
    slice x5 -> x0, local copies, waits for them, and re-layouts: 2.89 us -> none  [the longest x1 2.09 us: on_device(): before = passed_along(framed[:, frames - history:, :], 'tm', 1)]
    reshape x1 -> x0, local copies, waits for them, and re-layouts: 2.49 us -> none  [on_device(): framed = voltages.reshape(in_dev, frames, frame_len)]
  transfers between devices with their start and end apart: 1 -> 0, of which waited for: 1 -> 0; matrix products, arithmetic and copies ran while one was open for 1% -> 0% of each run, Pallas kernels for 0% -> 0%
where the time goes in v1:
time: 43.9 us; the launch traced here: 43.7 us
  Pallas kernels  39.7 us (90%)
  local copies, waits for them, and re-layouts  3.98 us (9%)
    pallas_call x1, Pallas kernels, on_device_fast(): pl.pallas_call(functools.partial(spectra_kernel, n_time, n_station, frame...  34.5 us
    pallas_call x1, Pallas kernels, on_device_fast(): pl.pallas_call(functools.partial(correlate_kernel, n_time), grid=(per_dev...  5.16 us
    unnamed x6, local copies, waits for them, and re-layouts  3.98 us

profile of v1, /device:TPU:0, one launch (start us, length us, event | category | flops | bytes accessed | tf_op | source)
XLA Modules:
  0.0 43.7 jit_solution(2522485404977366586)
XLA Ops:
  0.0 0.0 copy-start
  0.0 2.2 %copy-done = bf16[32,65536]{1,0:T(8,128)(2,1)S(1)} copy-done((bf16[32,65536]{1,0:T(8,128)(2,1)S(1)}, bf16[32,65536]{1,0:T(8,128)(2,1)}, u32[]{:S(2)}) %copy-start) | copy-done | bytes 4194328
  2.2 0.0 copy-start.1
  2.2 0.9 %copy-done.1 = f32[2,8,4096]{2,1,0:T(8,128)S(1)} copy-done((f32[2,8,4096]{2,1,0:T(8,128)S(1)}, f32[2,8,4096]{2,1,0:T(8,128)}, u32[]{:S(2)}) %copy-start.1) | copy-done | bytes 262168
  3.1 0.0 copy-start.2
  3.1 0.8 %copy-done.2 = f32[2,32,256]{2,1,0:T(8,128)S(1)} copy-done((f32[2,32,256]{2,1,0:T(8,128)S(1)}, f32[2,32,256]{2,1,0:T(8,128)}, u32[]{:S(2)}) %copy-start.2) | copy-done | bytes 65560
  4.0 34.5 %spectra.1 = bf16[32,32,128]{2,1,0:T(8,128)(2,1)S(1)} custom-call(bf16[32,65536]{1,0:T(8,128)(2,1)S(1)} %copy-done, f32[2,8,4096]{2,1,0:T(8,128)S(1)} %copy-done.1, bf16[2,2,4096,256]{3,2,1,0:T(8,128)(2,1)} %constant.5.clone.t_hbm, f32[2,32,256]{2,1,0:T(8,128)S(1)} %copy-done.2), custom_call_target="tpu_custom_call" | custom-call | tf_op jit(solution)/shard_map/spectra/pallas_call | solution.py:397
  38.5 5.2 %correlate.1 = f32[8,2,256,256]{3,2,1,0:T(8,128)} custom-call(bf16[1024,128]{1,0:T(8,128)(2,1)S(1)} %bitcast.1), custom_call_target="tpu_custom_call" | custom-call | tf_op jit(solution)/shard_map/correlate/pallas_call | solution.py:426
Async XLA Ops:
  0.0 2.2 %copy-start = (bf16[32,65536]{1,0:T(8,128)(2,1)S(1)}, bf16[32,65536]{1,0:T(8,128)(2,1)}, u32[]{:S(2)}) copy-start(bf16[32,65536]{1,0:T(8,128)(2,1)} %v_hbm.1) | copy-start | bytes 12582916
  2.2 0.9 %copy-start.1 = (f32[2,8,4096]{2,1,0:T(8,128)S(1)}, f32[2,8,4096]{2,1,0:T(8,128)}, u32[]{:S(2)}) copy-start(f32[2,8,4096]{2,1,0:T(8,128)} %constant.4.clone.w_hbm) | copy-start | bytes 786436
  3.1 0.8 %copy-start.2 = (f32[2,32,256]{2,1,0:T(8,128)S(1)}, f32[2,32,256]{2,1,0:T(8,128)}, u32[]{:S(2)}) copy-start(f32[2,32,256]{2,1,0:T(8,128)} %g_ref.1) | copy-start | bytes 196612

commit v2 on v1

v2 whole, which is shorter than its diff:
```python
import functools

import jax
import jax.numpy as jnp
import numpy as np
from jax import lax
from jax.experimental import pallas as pl
from jax.experimental.pallas import tpu as pltpu
from jax.sharding import PartitionSpec as P

CHANNELS = 4096
BAND_LOW = 1024
TAPS = 8


def passed_along(x, axis, by):
    devices = lax.axis_size(axis)
    pairs = [(i, i + by) for i in range(devices) if 0 <= i + by < devices]
    return lax.ppermute(x, axis, pairs)


def window_table(chans):
    frame_len = 2 * chans
    total_len = TAPS * frame_len
    positions = jnp.arange(total_len, dtype=jnp.float32)
    centred = (positions - (total_len - 1) / 2.0) / frame_len
    taper = jnp.sin(jnp.pi * (positions + 0.5) / total_len)
    shaped = jnp.sinc(centred) * taper * taper
    shaped = shaped / jnp.sqrt(jnp.sum(shaped * shaped))
    return shaped.reshape(TAPS, frame_len)


def band_tables(frame_len, band):
    sample_index = jnp.arange(frame_len, dtype=jnp.int32)[:, None]
    channel_index = (BAND_LOW + jnp.arange(band, dtype=jnp.int32))[None, :]
    phase = (sample_index * channel_index % frame_len).astype(jnp.float32)
    angles = 2.0 * jnp.pi * phase / frame_len
    return (jnp.cos(angles), jnp.sin(angles))


def band_spectra(windowed, cos_table, sin_table):
    highest = lax.Precision.HIGHEST
    real_part = jnp.einsum("ifm,mk->kif", windowed, cos_table, precision=highest)
    imag_part = -jnp.einsum("ifm,mk->kif", windowed, sin_table, precision=highest)
    return (real_part, imag_part)


def apply_taps(window, extended, frames):
    windowed = jnp.zeros((extended.shape[0], frames, extended.shape[2]), jnp.float32)
    for tap_index in range(TAPS):
        windowed = windowed + window[tap_index] * extended[
            :, tap_index : tap_index + frames, :
        ].astype(jnp.float32)
    return windowed


def operands(turned):
    stacked = jnp.concatenate([turned[0], turned[1]], axis=-1)
    flipped = jnp.concatenate([turned[1], -turned[0]], axis=-1)
    return (stacked, flipped)


def cross_power(stacked, flipped, total_frames):
    vis_real = jnp.einsum("cif,cjf->cij", stacked, stacked, preferred_element_type=jnp.float32)
    vis_imag = jnp.einsum("cif,cjf->cij", flipped, stacked, preferred_element_type=jnp.float32)
    return jnp.stack([vis_real, vis_imag], axis=1) / total_frames


def on_device(voltages, gains):
    in_dev, length = voltages.shape
    band = gains.shape[2]
    frame_len = 2 * CHANNELS
    frames = length // frame_len
    n_time = lax.axis_size("tm")
    n_station = lax.axis_size("stn")
    per_device = band // (n_time * n_station)
    all_inputs = in_dev * n_station
    history = TAPS - 1
    window = window_table(CHANNELS)
    cos_table, sin_table = band_tables(frame_len, band)
    framed = voltages.reshape(in_dev, frames, frame_len)
    before = passed_along(framed[:, frames - history :, :], "tm", 1)
    extended = jnp.concatenate([before, framed], axis=1)
    windowed = apply_taps(window, extended, frames)
    raw_real, raw_imag = band_spectra(windowed, cos_table, sin_table)
    gain_real = jnp.transpose(gains[0])[:, :, None]
    gain_imag = jnp.transpose(gains[1])[:, :, None]
    spec_real = gain_real * raw_real - gain_imag * raw_imag
    spec_imag = gain_real * raw_imag + gain_imag * raw_real
    spectra = jnp.stack([spec_real, spec_imag]).astype(jnp.bfloat16)
    blocks = spectra.reshape(2, n_time, n_station, per_device, in_dev, frames)
    turned = lax.all_to_all(
        lax.all_to_all(blocks, "tm", split_axis=1, concat_axis=5, tiled=True),
        "stn",
        split_axis=2,
        concat_axis=4,
        tiled=True,
    )
    turned = turned.reshape(2, per_device, all_inputs, n_time * frames)
    stacked, flipped = operands(turned)
    return cross_power(stacked, flipped, float(n_time * frames))


CHUNK = 512
LANES = 128


def host_window(chans):
    frame_len = 2 * chans
    total = TAPS * frame_len
    n = np.arange(total, dtype=np.float64)
    raw = np.sinc((n - (total - 1) / 2) / frame_len)
    raw = raw * np.sin(np.pi * (n + 0.5) / total) ** 2
    return (raw / np.sqrt(np.sum(raw * raw))).reshape(TAPS, frame_len).astype(np.float32)


def host_tables(chans, band, owners):
    frame_len = 2 * chans
    m = np.arange(chans, dtype=np.int64)[:, None]
    parts = []
    for parity in range(2):
        c = BAND_LOW + np.arange(parity, band, 2, dtype=np.int64)[None, :]
        angle = 2.0 * np.pi * ((m * c) % frame_len) / frame_len
        parts.append(np.concatenate([np.cos(angle), -np.sin(angle)], axis=1))
    full = np.stack(parts)
    high = full.astype(np.float32).astype(jnp.bfloat16)
    low = (full - high.astype(np.float64)).astype(np.float32).astype(jnp.bfloat16)
    return np.stack([high, low])


def taps_into(v_ref, w_ref, x_ref, base, in_dev, frames, halo):
    rows = in_dev * (frames - 1 if halo else frames)
    for tile in range(CHUNK // LANES):
        at = pl.multiple_of(base + tile * LANES, LANES)
        for part in range(in_dev // 16):
            who = slice(part * 16, part * 16 + 16)
            halves = []
            for half in range(2):
                v = [
                    v_ref[2 * f + half, who, pl.ds(at, LANES)].astype(jnp.float32)
                    for f in range(frames)
                ]
                w = [w_ref[half, pl.ds(p, 1), pl.ds(at, LANES)] for p in range(TAPS)]
                sums = []
                if halo:
                    for j in range(frames - 1):
                        sums.append(sum(w[p] * v[j + 1 + p] for p in range(TAPS - 1 - j)))
                else:
                    for f in range(frames):
                        sums.append(sum(w[TAPS - 1 - q] * v[f - q] for q in range(f + 1)))
                halves.append(sums)
            for f in range(len(halves[0])):
                for parity in range(2):
                    a, b = halves[0][f], halves[1][f]
                    x = a - b if parity else a + b
                    high = x.astype(jnp.bfloat16)
                    low = (x - high.astype(jnp.float32)).astype(jnp.bfloat16)
                    r = f * in_dev + part * 16
                    x_ref[parity, r : r + 16, pl.ds(at, LANES)] = high
                    x_ref[parity, rows + r : rows + r + 16, pl.ds(at, LANES)] = low


def transform(x_ref, t_ref, acc_ref, parity, base, depth, rows):
    at = pl.ds(pl.multiple_of(base, depth), depth)
    x = x_ref[parity, 0 : 2 * rows, at]
    both = jnp.dot(x, t_ref[0, parity, at, :], preferred_element_type=jnp.float32)
    extra = jnp.dot(x[:rows], t_ref[1, parity, at, :], preferred_element_type=jnp.float32)
    acc_ref[parity] += both[:rows] + both[rows:] + extra


def swap_blocks(arrays, block):
    lane = lax.broadcasted_iota(jnp.int32, arrays[0].shape, 1)
    step = 1
    while step < len(arrays):
        low = (lane // (block * step)) % 2 == 0
        shift = block * step
        out = list(arrays)
        for q in range(len(arrays)):
            if q & step == 0:
                a, b = arrays[q], arrays[q | step]
                out[q] = jnp.where(low, a, pltpu.roll(b, shift, 1))
                out[q | step] = jnp.where(low, pltpu.roll(a, LANES - shift, 1), b)
        arrays = out
        step *= 2
    return arrays


def spectra_kernel(
    n_time, n_station, frames,
    v_hbm, w_hbm, t_hbm, g_ref, got_ref,
    v_ref, w_ref, t_ref, hx, x, hacc, acc, hrecv, send, gain,
    v_sem, w_sem, t_sem, hs_sem, hr_sem, send_sem, recv_sem,
):
    me_t, me_s = lax.axis_index("tm"), lax.axis_index("stn")
    n_dev = n_time * n_station
    me = me_t * n_station + me_s
    in_dev, half_len = v_ref.shape[1], v_ref.shape[2]
    chunks = half_len // CHUNK
    rows, hrows = in_dev * frames, in_dev * (frames - 1)
    first = 2 * CHUNK
    spans = (slice(0, first), slice(first, half_len))

    def v_copy(g, i):
        return pltpu.make_async_copy(
            v_hbm.at[:, i * half_len + spans[g].start : i * half_len + spans[g].stop],
            v_ref.at[i, :, spans[g]],
            v_sem.at[g, i],
        )

    def t_copy(g, parity):
        return pltpu.make_async_copy(
            t_hbm.at[:, parity, spans[g], :], t_ref.at[:, parity, spans[g], :], t_sem.at[g, parity]
        )

    w_copy = pltpu.make_async_copy(w_hbm, w_ref, w_sem)
    w_copy.start()
    for g in range(2):
        for i in range(2 * frames):
            v_copy(g, i).start()
        t_copy(g, 0).start()
    for g in range(2):
        t_copy(g, 1).start()

    barrier = pltpu.get_barrier_semaphore()

    def greet(o, carry):
        to = lax.rem(me + o, n_dev)
        pl.semaphore_signal(
            barrier, inc=1, device_id=(to // n_station, lax.rem(to, n_station)),
            device_id_type=pl.DeviceIdType.MESH,
        )
        return carry

    lax.fori_loop(1, n_dev, greet, 0)
    hacc[...] = jnp.zeros_like(hacc)
    acc[...] = jnp.zeros_like(acc)

    band = g_ref.shape[2]
    half = band // 2
    row = lax.broadcasted_iota(jnp.int32, (band, band), 0)
    col = lax.broadcasted_iota(jnp.int32, (band, band), 1)
    pick = (row == 2 * lax.rem(col, half) + col // half).astype(jnp.float32)
    for reim in range(2):
        gain[reim] = jnp.dot(
            g_ref[reim], pick, precision=lax.Precision.HIGHEST, preferred_element_type=jnp.float32
        )

    def arrived(g):
        for i in range(2 * frames):
            v_copy(g, i).wait()
        t_copy(g, 0).wait()

    def taps(c, halo):
        taps_into(v_ref, w_ref, hx if halo else x, c * CHUNK, in_dev, frames, halo)

    def onward(parity):
        return pltpu.make_async_remote_copy(
            src_ref=hacc.at[parity], dst_ref=hrecv.at[parity],
            send_sem=hs_sem.at[parity], recv_sem=hr_sem.at[parity],
            device_id=(lax.rem(me_t + 1, n_time), me_s), device_id_type=pl.DeviceIdType.MESH,
        )

    def pass_on(parity):
        @pl.when(me_t < n_time - 1)
        def _():
            onward(parity).start()

    def outgoing(parity, o):
        to = lax.rem(me + o, n_dev)
        return pltpu.make_async_remote_copy(
            src_ref=send.at[parity, to], dst_ref=got_ref.at[parity, me],
            send_sem=send_sem.at[parity, o], recv_sem=recv_sem.at[parity, me],
            device_id=(to // n_station, lax.rem(to, n_station)),
            device_id_type=pl.DeviceIdType.MESH,
        )

    def incoming(parity, o):
        src = lax.rem(me + o, n_dev)
        return pltpu.make_async_remote_copy(
            src_ref=send.at[parity, src], dst_ref=got_ref.at[parity, src],
            send_sem=send_sem.at[parity, o], recv_sem=recv_sem.at[parity, src],
            device_id=(src // n_station, lax.rem(src, n_station)),
            device_id_type=pl.DeviceIdType.MESH,
        )

    def hand_out(parity):
        @pl.when(me_t > 0)
        def _():
            onward(parity).wait_recv()
            acc[parity, 0:hrows, :] += hrecv[parity]

        arrays = []
        for part in range(in_dev // 16):
            who = slice(part * 16, part * 16 + 16)
            gr = gain[0, who, parity * half : (parity + 1) * half]
            gi = gain[1, who, parity * half : (parity + 1) * half]
            res, ims = [], []
            for f in range(frames):
                r = f * in_dev + part * 16
                re = acc[parity, r : r + 16, 0:half]
                im = acc[parity, r : r + 16, half:band]
                res.append(gr * re - gi * im)
                ims.append(gr * im + gi * re)
            arrays += res + ims
        arrays = swap_blocks(arrays, LANES // len(arrays))
        for d in range(n_dev):
            send[parity, d] = arrays[d].astype(jnp.bfloat16)
        lax.fori_loop(1, n_dev, lambda o, k: (outgoing(parity, o).start(), k)[1], 0)
        got_ref[parity, me] = send[parity, me]

    w_copy.wait()
    arrived(0)
    taps(0, True)
    taps(1, True)
    transform(hx, t_ref, hacc, 0, 0, CHUNK, hrows)
    arrived(1)

    def stage(c, carry):
        taps(c + 1, True)
        transform(hx, t_ref, hacc, 0, c * CHUNK, CHUNK, hrows)
        return carry

    lax.fori_loop(1, chunks - 1, stage, 0)
    transform(hx, t_ref, hacc, 0, (chunks - 1) * CHUNK, CHUNK, hrows)
    pl.semaphore_wait(barrier, n_dev - 1)
    pass_on(0)
    for g in range(2):
        t_copy(g, 1).wait()

    def stage_odd(c, carry):
        taps(c, False)
        transform(hx, t_ref, hacc, 1, c * CHUNK, CHUNK, hrows)
        return carry

    lax.fori_loop(0, chunks, stage_odd, 0)
    pass_on(1)
    for parity in range(2):

        def own(c, carry):
            transform(x, t_ref, acc, parity, c * 2 * CHUNK, 2 * CHUNK, rows)
            return carry

        lax.fori_loop(0, chunks // 2, own, 0)
        hand_out(parity)

    for parity in range(2):
        lax.fori_loop(1, n_dev, lambda o, k: (incoming(parity, o).wait_recv(), k)[1], 0)
        lax.fori_loop(1, n_dev, lambda o, k: (outgoing(parity, o).wait_send(), k)[1], 0)

        @pl.when(me_t < n_time - 1)
        def _():
            onward(parity).wait_send()


def correlate_kernel(n_time, n_station, got_ref, out_hbm, a_ref, out_ref, out_sem):
    inputs = out_ref.shape[2]
    group = 16
    side, reach = LANES // 2, LANES // 4
    wide_shape = (n_station * group, LANES)
    lane = lax.broadcasted_iota(jnp.int32, wide_shape, 1)
    is_low, is_real = lane < side, (lane // reach) % 2 == 0
    scale = 1.0 / (TAPS * n_time)
    copies = []
    for parity in range(2):
        for two in range(n_time // 2):
            g0, g1 = [
                got_ref[parity, t * n_station : (t + 1) * n_station]
                .astype(jnp.float32)
                .reshape(wide_shape)
                for t in (2 * two, 2 * two + 1)
            ]
            here = slice(two * LANES, (two + 1) * LANES)
            for part in range(2):
                if part == 0:
                    a = jnp.where(is_low, g0, pltpu.roll(g1, side, 1))
                else:
                    a = jnp.where(is_low, pltpu.roll(g0, side, 1), g1)
                turned = jnp.where(
                    is_real, pltpu.roll(a, LANES - reach, 1), -pltpu.roll(a, reach, 1)
                )
                for i, rows in ((0, a), (inputs, turned)):
                    rows = rows.astype(jnp.bfloat16)
                    for s in range(n_station):
                        to = i + (2 * s + part) * group
                        a_ref[parity, to : to + group, here] = rows[s * group : (s + 1) * group]
        width = n_time * side
        pair = lax.rem(lax.broadcasted_iota(jnp.int32, (1, width), 1), 4)
        for u in range(out_ref.shape[0] // 2):
            mask = jnp.where(pair == u, scale, 0.0).astype(jnp.bfloat16)
            power = lax.dot_general(
                a_ref[parity], a_ref[parity, 0:inputs, :] * mask, (((1,), (1,)), ((), ())),
                preferred_element_type=jnp.float32,
            )
            c = 2 * u + parity
            out_ref[c, 0] = power[:inputs]
            out_ref[c, 1] = power[inputs:]
            copy = pltpu.make_async_copy(out_ref.at[c], out_hbm.at[c], out_sem.at[c])
            copy.start()
            copies.append(copy)
    for copy in copies:
        copy.wait()


def on_device_fast(voltages, gains):
    in_dev, length = voltages.shape
    band = gains.shape[2]
    frame_len = 2 * CHANNELS
    frames = length // frame_len
    n_time = lax.axis_size("tm")
    n_station = lax.axis_size("stn")
    n_dev = n_time * n_station
    inputs = in_dev * n_station
    hrows = in_dev * (frames - 1)
    rows = in_dev * frames
    window = host_window(CHANNELS).reshape(TAPS, 2, CHANNELS).transpose(1, 0, 2)
    tables = host_tables(CHANNELS, band, n_dev)
    any_space = pl.BlockSpec(memory_space=pl.ANY)
    vmem = pl.BlockSpec(memory_space=pltpu.VMEM)
    got = pl.pallas_call(
        functools.partial(spectra_kernel, n_time, n_station, frames),
        out_shape=jax.ShapeDtypeStruct((2, n_dev, in_dev // 2, LANES), jnp.bfloat16),
        in_specs=[any_space, any_space, any_space, vmem],
        out_specs=vmem,
        scratch_shapes=[
            pltpu.VMEM((2 * frames, in_dev, CHANNELS), jnp.bfloat16),
            pltpu.VMEM((2, TAPS, CHANNELS), jnp.float32),
            pltpu.VMEM((2, 2, CHANNELS, band), jnp.bfloat16),
            pltpu.VMEM((2, 2 * hrows, CHANNELS), jnp.bfloat16),
            pltpu.VMEM((2, 2 * rows, CHANNELS), jnp.bfloat16),
            pltpu.VMEM((2, hrows, band), jnp.float32),
            pltpu.VMEM((2, rows, band), jnp.float32),
            pltpu.VMEM((2, hrows, band), jnp.float32),
            pltpu.VMEM((2, n_dev, in_dev // 2, LANES), jnp.bfloat16),
            pltpu.VMEM((2, in_dev, band), jnp.float32),
            pltpu.SemaphoreType.DMA((2, 2 * frames)),
            pltpu.SemaphoreType.DMA,
            pltpu.SemaphoreType.DMA((2, 2)),
            pltpu.SemaphoreType.DMA((2,)),
            pltpu.SemaphoreType.DMA((2,)),
            pltpu.SemaphoreType.DMA((2, n_dev)),
            pltpu.SemaphoreType.DMA((2, n_dev)),
        ],
        compiler_params=pltpu.CompilerParams(
            collective_id=0, has_side_effects=True, vmem_limit_bytes=61 * 2**20
        ),
        name="spectra",
    )(voltages, window, tables, gains)
    per_device = band // n_dev
    return pl.pallas_call(
        functools.partial(correlate_kernel, n_time, n_station),
        out_shape=jax.ShapeDtypeStruct((per_device, 2, inputs, inputs), jnp.float32),
        in_specs=[vmem],
        out_specs=any_space,
        scratch_shapes=[
            pltpu.VMEM((2, 2 * inputs, n_time * LANES // 2), jnp.bfloat16),
            pltpu.VMEM((per_device, 2, inputs, inputs), jnp.float32),
            pltpu.SemaphoreType.DMA((per_device,)),
        ],
        compiler_params=pltpu.CompilerParams(vmem_limit_bytes=48 * 2**20),
        name="correlate",
    )(got)


def solution(mesh):
    in_specs = (P("stn", "tm"), P(None, "stn", None))
    out_specs = P(("tm", "stn"), None, None, None)

    def body(voltages, gains):
        n_dev = mesh.shape["tm"] * mesh.shape["stn"]
        frames = voltages.shape[1] // (2 * CHANNELS)
        if 2 * frames * (gains.shape[2] // n_dev) == LANES and frames == TAPS and voltages.shape[0] == 32:
            return on_device_fast(voltages, gains)
        return on_device(voltages, gains)

    return jax.shard_map(
        body, mesh=mesh, in_specs=in_specs, out_specs=out_specs, check_vma=False
    )
```

time: 43.9 us -> 42.7 us (0.973)
  local copies, waits for them, and re-layouts: 3.98 us -> 0.94 us
  Pallas kernels: 39.7 us -> 41.5 us
    pallas_call x1, Pallas kernels: 34.5 us -> 39 us  [on_device_fast(): pl.pallas_call(functools.partial(spectra_kernel, n_time, n_station, frame...]
    unnamed x6 -> x2, local copies, waits for them, and re-layouts: 3.98 us -> 0.94 us
    pallas_call x1, Pallas kernels: 5.16 us -> 2.51 us  [on_device_fast(): pl.pallas_call(functools.partial(correlate_kernel, n_time, n_station), ou...]
where the time goes in v2:
time: 42.7 us; the launch traced here: 42.5 us
  Pallas kernels  41.5 us (97%)
  local copies, waits for them, and re-layouts  0.94 us (2%)
    pallas_call x1, Pallas kernels, on_device_fast(): pl.pallas_call(functools.partial(spectra_kernel, n_time, n_station, frame...  39 us
    pallas_call x1, Pallas kernels, on_device_fast(): pl.pallas_call(functools.partial(correlate_kernel, n_time, n_station), ou...  2.51 us
    unnamed x2, local copies, waits for them, and re-layouts  0.94 us

profile of v2, /device:TPU:0, one launch (start us, length us, event | category | flops | bytes accessed | tf_op | source)
XLA Modules:
  0.0 42.5 jit_solution(16696328148680007491)
XLA Ops:
  0.0 39.0 %spectra.1.got_ref = bf16[2,32,16,128]{3,2,1,0:T(8,128)(2,1)} custom-call(bf16[32,65536]{1,0:T(8,128)(2,1)} %v_hbm.1, f32[2,8,4096]{2,1,0:T(8,128)} %constant.4.clone.w_hbm, bf16[2,2,4096,256]{3,2,1,0:T(8,128)(2,1)} %constant.5.clone.t_hbm, f32[2,32,256]{2,1,0:T(8,128)} %g_ref.1), custom_call_target="tpu_custom_call" | custom-call | tf_op jit(solution)/shard_map/spectra/pallas_call | solution.py:419
  39.0 0.0 copy-start
  39.0 0.9 %copy-done = bf16[2,32,16,128]{3,2,1,0:T(8,128)(2,1)S(1)} copy-done((bf16[2,32,16,128]{3,2,1,0:T(8,128)(2,1)S(1)}, bf16[2,32,16,128]{3,2,1,0:T(8,128)(2,1)}, u32[]{:S(2)}) %copy-start) | copy-done | bytes 262168
  40.0 2.5 %correlate.1 = f32[8,2,256,256]{3,2,1,0:T(8,128)} custom-call(bf16[2,32,16,128]{3,2,1,0:T(8,128)(2,1)S(1)} %copy-done), custom_call_target="tpu_custom_call" | custom-call | tf_op jit(solution)/shard_map/correlate/pallas_call | solution.py:449
Async XLA Ops:
  39.0 1.0 %copy-start = (bf16[2,32,16,128]{3,2,1,0:T(8,128)(2,1)S(1)}, bf16[2,32,16,128]{3,2,1,0:T(8,128)(2,1)}, u32[]{:S(2)}) copy-start(bf16[2,32,16,128]{3,2,1,0:T(8,128)(2,1)} %spectra.1.got_ref) | copy-start | bytes 786436

commit v3 on v2

--- a/solution.py
+++ b/solution.py
@@ -132,6 +132,7 @@
     rows = in_dev * (frames - 1 if halo else frames)
     for tile in range(CHUNK // LANES):
         at = pl.multiple_of(base + tile * LANES, LANES)
+        into = slice(tile * LANES, (tile + 1) * LANES)
         for part in range(in_dev // 16):
             who = slice(part * 16, part * 16 + 16)
             halves = []
@@ -156,13 +157,13 @@
                     high = x.astype(jnp.bfloat16)
                     low = (x - high.astype(jnp.float32)).astype(jnp.bfloat16)
                     r = f * in_dev + part * 16
-                    x_ref[parity, r : r + 16, pl.ds(at, LANES)] = high
-                    x_ref[parity, rows + r : rows + r + 16, pl.ds(at, LANES)] = low
+                    x_ref[parity, r : r + 16, into] = high
+                    x_ref[parity, rows + r : rows + r + 16, into] = low
 
 
 def transform(x_ref, t_ref, acc_ref, parity, base, depth, rows):
     at = pl.ds(pl.multiple_of(base, depth), depth)
-    x = x_ref[parity, 0 : 2 * rows, at]
+    x = x_ref[parity]
     both = jnp.dot(x, t_ref[0, parity, at, :], preferred_element_type=jnp.float32)
     extra = jnp.dot(x[:rows], t_ref[1, parity, at, :], preferred_element_type=jnp.float32)
     acc_ref[parity] += both[:rows] + both[rows:] + extra
@@ -188,7 +189,7 @@
 def spectra_kernel(
     n_time, n_station, frames,
     v_hbm, w_hbm, t_hbm, g_ref, got_ref,
-    v_ref, w_ref, t_ref, hx, x, hacc, acc, hrecv, send, gain,
+    v_ref, w_ref, t_ref, hx0, hx1, x, hacc, acc, hrecv, send, gain,
     v_sem, w_sem, t_sem, hs_sem, hr_sem, send_sem, recv_sem,
 ):
     me_t, me_s = lax.axis_index("tm"), lax.axis_index("stn")
@@ -250,8 +251,17 @@
             v_copy(g, i).wait()
         t_copy(g, 0).wait()
 
-    def taps(c, halo):
-        taps_into(v_ref, w_ref, hx if halo else x, c * CHUNK, in_dev, frames, halo)
+    def taps(c):
+        taps_into(v_ref, w_ref, x.at[c], c * CHUNK, in_dev, frames, False)
+
+    def halo_taps(k, odd):
+        taps_into(
+            v_ref, w_ref, (hx0, hx1)[odd].at[k], (2 * k + odd) * CHUNK, in_dev, frames, True
+        )
+
+    def halo_dots(parity, k, odd):
+        c = (2 * k + odd) * CHUNK
+        transform((hx0, hx1)[odd].at[k], t_ref, hacc, parity, c, CHUNK, hrows)
 
     def onward(parity):
         return pltpu.make_async_remote_copy(
@@ -310,37 +320,40 @@
 
     w_copy.wait()
     arrived(0)
-    taps(0, True)
-    taps(1, True)
-    transform(hx, t_ref, hacc, 0, 0, CHUNK, hrows)
+    halo_taps(0, 0)
+    halo_taps(0, 1)
+    halo_dots(0, 0, 0)
     arrived(1)
 
-    def stage(c, carry):
-        taps(c + 1, True)
-        transform(hx, t_ref, hacc, 0, c * CHUNK, CHUNK, hrows)
+    def stage(k, carry):
+        halo_taps(k, 0)
+        halo_dots(0, k - 1, 1)
+        halo_taps(k, 1)
+        halo_dots(0, k, 0)
         return carry
 
-    lax.fori_loop(1, chunks - 1, stage, 0)
-    transform(hx, t_ref, hacc, 0, (chunks - 1) * CHUNK, CHUNK, hrows)
+    lax.fori_loop(1, chunks // 2, stage, 0)
+    halo_dots(0, chunks // 2 - 1, 1)
     pl.semaphore_wait(barrier, n_dev - 1)
     pass_on(0)
     for g in range(2):
         t_copy(g, 1).wait()
 
-    def stage_odd(c, carry):
-        taps(c, False)
-        transform(hx, t_ref, hacc, 1, c * CHUNK, CHUNK, hrows)
+    def stage_odd(k, carry):
+        for odd in range(2):
+            taps(2 * k + odd)
+            halo_dots(1, k, odd)
         return carry
 
-    lax.fori_loop(0, chunks, stage_odd, 0)
+    lax.fori_loop(0, chunks // 2, stage_odd, 0)
     pass_on(1)
     for parity in range(2):
 
         def own(c, carry):
-            transform(x, t_ref, acc, parity, c * 2 * CHUNK, 2 * CHUNK, rows)
+            transform(x.at[c], t_ref, acc, parity, c * CHUNK, CHUNK, rows)
             return carry
 
-        lax.fori_loop(0, chunks // 2, own, 0)
+        lax.fori_loop(0, chunks, own, 0)
         hand_out(parity)
 
     for parity in range(2):
@@ -425,8 +438,9 @@
             pltpu.VMEM((2 * frames, in_dev, CHANNELS), jnp.bfloat16),
             pltpu.VMEM((2, TAPS, CHANNELS), jnp.float32),
             pltpu.VMEM((2, 2, CHANNELS, band), jnp.bfloat16),
-            pltpu.VMEM((2, 2 * hrows, CHANNELS), jnp.bfloat16),
-            pltpu.VMEM((2, 2 * rows, CHANNELS), jnp.bfloat16),
+            pltpu.VMEM((CHANNELS // CHUNK // 2, 2, 2 * hrows, CHUNK), jnp.bfloat16),
+            pltpu.VMEM((CHANNELS // CHUNK // 2, 2, 2 * hrows, CHUNK), jnp.bfloat16),
+            pltpu.VMEM((CHANNELS // CHUNK, 2, 2 * rows, CHUNK), jnp.bfloat16),
             pltpu.VMEM((2, hrows, band), jnp.float32),
             pltpu.VMEM((2, rows, band), jnp.float32),
             pltpu.VMEM((2, hrows, band), jnp.float32),

time: 42.7 us -> 37.4 us (0.88)
  Pallas kernels: 41.5 us -> 36.3 us
    pallas_call x1, Pallas kernels: 39 us -> 33.7 us  [on_device_fast(): pl.pallas_call(functools.partial(spectra_kernel, n_time, n_station, frame...]
where the time goes in v3:
time: 37.4 us; the launch traced here: 37.2 us
  Pallas kernels  36.3 us (97%)
  local copies, waits for them, and re-layouts  0.94 us (3%)
    pallas_call x1, Pallas kernels, on_device_fast(): pl.pallas_call(functools.partial(spectra_kernel, n_time, n_station, frame...  33.7 us
    pallas_call x1, Pallas kernels, on_device_fast(): pl.pallas_call(functools.partial(correlate_kernel, n_time, n_station), ou...  2.51 us
    unnamed x2, local copies, waits for them, and re-layouts  0.94 us

profile of v3, /device:TPU:0, one launch (start us, length us, event | category | flops | bytes accessed | tf_op | source)
XLA Modules:
  0.0 37.2 jit_solution(6508624887113707784)
XLA Ops:
  0.0 33.7 %spectra.1.got_ref = bf16[2,32,16,128]{3,2,1,0:T(8,128)(2,1)} custom-call(bf16[32,65536]{1,0:T(8,128)(2,1)} %v_hbm.1, f32[2,8,4096]{2,1,0:T(8,128)} %constant.4.clone.w_hbm, bf16[2,2,4096,256]{3,2,1,0:T(8,128)(2,1)} %constant.5.clone.t_hbm, f32[2,32,256]{2,1,0:T(8,128)} %g_ref.1), custom_call_target="tpu_custom_call" | custom-call | tf_op jit(solution)/shard_map/spectra/pallas_call | solution.py:432
  33.7 0.0 copy-start
  33.8 0.9 %copy-done = bf16[2,32,16,128]{3,2,1,0:T(8,128)(2,1)S(1)} copy-done((bf16[2,32,16,128]{3,2,1,0:T(8,128)(2,1)S(1)}, bf16[2,32,16,128]{3,2,1,0:T(8,128)(2,1)}, u32[]{:S(2)}) %copy-start) | copy-done | bytes 262168
  34.7 2.5 %correlate.1 = f32[8,2,256,256]{3,2,1,0:T(8,128)} custom-call(bf16[2,32,16,128]{3,2,1,0:T(8,128)(2,1)S(1)} %copy-done), custom_call_target="tpu_custom_call" | custom-call | tf_op jit(solution)/shard_map/correlate/pallas_call | solution.py:463
Async XLA Ops:
  33.7 1.0 %copy-start = (bf16[2,32,16,128]{3,2,1,0:T(8,128)(2,1)S(1)}, bf16[2,32,16,128]{3,2,1,0:T(8,128)(2,1)}, u32[]{:S(2)}) copy-start(bf16[2,32,16,128]{3,2,1,0:T(8,128)(2,1)} %spectra.1.got_ref) | copy-start | bytes 786436
